TPU v7x, 32 devices: a whole 2x2x4 slice. The times are simulated.
32 devices in a mesh: pos: 16 (over z, y, x), val: 2 (over core).
Axes of the slice: x: 2, y: 2, z: 4, core: 2. Of those that a mesh axis runs over, the one named last changes fastest.
Arguments:
- send_load: int32 [2, 16], replicated, may hold values from 1 to 16, 64 in all within a row
- tokens: int32 [2, 256, 81], P('val', 'pos'), may hold values from 0 to 63
- owner: int32 [2, 256], P('val', 'pos'), may hold values from 0 to 15
- joint_action: int32 [2, 256, 7], P('val', 'pos'), may hold values from 0 to 31
- board_context: bfloat16 [32, 81, 512], P('pos'), may hold values from -6 to 6
- tok_embed: bfloat16 [64, 512], replicated, may hold values from -6 to 6
- w_qkv: bfloat16 [512, 1536], replicated, may hold values from -0.25 to 0.25
- w_attn_out: bfloat16 [512, 512], replicated, may hold values from -0.25 to 0.25
- w_up: bfloat16 [512, 1024], replicated, may hold values from -0.25 to 0.25
- w_down: bfloat16 [1024, 512], replicated, may hold values from -0.1875 to 0.1875
- w_value: bfloat16 [512, 7], replicated, may hold values from -0.25 to 0.25
Outputs:
- state_values: float32 [2, 256, 7], P('val', 'pos')
- avg_policy: float32 [32, 7, 32], P('pos')
Inputs may be any that keep to these rules, and one draw needn't show every extreme that they name: Each row of send_load sums to 64, and its largest entry is exactly 16.
All inputs are finite; a program needn't handle non-finite values.
Results may differ from a plain program's by a relative error of at most 0.0055.
Values may be sent and summed in bfloat16 or wider, within the bound.
No kernel may reach another device: no remote copies, remote signals or barrier semaphores. Data moves between devices by JAX's collectives and lax.ppermute only.
A program may use at most 64 MiB of HBM per device.

v0:
```python
import jax
import jax.numpy as jnp
from jax import lax
from jax.sharding import PartitionSpec as P

HEADS = 8
POWERS = 7
ACTIONS = 32
ITERS = 8


smoothing = 0.01


def layer_norm(values):
    centre = values - jnp.mean(values, axis=-1, keepdims=True)
    spread = jnp.mean(centre * centre, axis=-1, keepdims=True)
    return centre * lax.rsqrt(spread + 1e-05)


def multiply(pattern, first_op, second_op):
    return jnp.einsum(pattern, first_op, second_op, preferred_element_type=jnp.float32)


def embed_tokens(token_ids, tok_embed):
    token_hot = (token_ids[..., None] == jnp.arange(tok_embed.shape[0], dtype=jnp.int32)).astype(
        jnp.bfloat16
    )
    return multiply("nlv,vd->nld", token_hot, tok_embed)


def build_states(token_ids, local_ids, tok_embed, board_context):
    local_hot = (
        local_ids[:, None] == jnp.arange(board_context.shape[0], dtype=jnp.int32)[None, :]
    ).astype(jnp.bfloat16)
    return embed_tokens(token_ids, tok_embed) + multiply("np,pld->nld", local_hot, board_context)


def encode(states, w_qkv, w_attn_out, w_up, w_down, w_value):
    batch_size, loc_count, model_width = states.shape
    head_size = model_width // HEADS
    inputs = states.astype(jnp.float32)
    normed = layer_norm(inputs).astype(jnp.bfloat16)
    joined = multiply("bld,de->ble", normed, w_qkv).astype(jnp.bfloat16)
    queries = joined[:, :, :model_width].reshape(batch_size, loc_count, HEADS, head_size)
    key_rows = joined[:, :, model_width : 2 * model_width].reshape(
        batch_size, loc_count, HEADS, head_size
    )
    value_rows = joined[:, :, 2 * model_width :].reshape(batch_size, loc_count, HEADS, head_size)
    scores = multiply("bqhe,bkhe->bhqk", queries, key_rows) * head_size ** (-0.5)
    weights = jnp.exp(scores)
    attention = (weights / jnp.sum(weights, axis=-1, keepdims=True)).astype(jnp.bfloat16)
    combined = (
        multiply("bhqk,bkhe->bqhe", attention, value_rows)
        .astype(jnp.bfloat16)
        .reshape(batch_size, loc_count, model_width)
    )
    hidden = inputs + multiply("bld,de->ble", combined, w_attn_out)
    normed_two = layer_norm(hidden).astype(jnp.bfloat16)
    activated = jax.nn.gelu(multiply("bld,df->blf", normed_two, w_up), approximate=True).astype(
        jnp.bfloat16
    )
    hidden = hidden + multiply("blf,fd->bld", activated, w_down)
    pooled = layer_norm(jnp.mean(hidden, axis=1)).astype(jnp.bfloat16)
    logits = 2.0 * jnp.dot(pooled, w_value, preferred_element_type=jnp.float32)
    raised = jnp.exp(logits)
    return raised / jnp.sum(raised, axis=-1, keepdims=True)


def regret_matching(value_sums, counts):
    visits = jnp.sum(counts, axis=-1, keepdims=True)
    totals = jnp.sum(value_sums, axis=-1, keepdims=True)
    baseline = (totals + 1.0 / POWERS) / (visits + 1.0)
    payoff = (value_sums + baseline) / (counts + 1.0)
    regrets = jnp.zeros_like(payoff[:, 0])
    average = jnp.zeros_like(payoff[:, 0])
    for iteration in range(ITERS):
        positive = jnp.maximum(regrets, 0.0)
        policy = (positive + smoothing) / (
            jnp.sum(positive, axis=-1, keepdims=True) + ACTIONS * smoothing
        )
        current = payoff[:, iteration]
        expected = jnp.sum(policy * current, axis=-1, keepdims=True)
        regrets = regrets + current - expected
        average = average + policy
    return average / ITERS


def local(
    send_load,
    tokens,
    owner,
    joint_action,
    board_context,
    tok_embed,
    w_qkv,
    w_attn_out,
    w_up,
    w_down,
    w_value,
):
    n_peers = lax.axis_size("pos")
    my_index = lax.axis_index("pos")
    val_index = lax.axis_index("val")
    evaluated = n_peers // 4
    slot_count = tokens.shape[1]
    local_positions = board_context.shape[0]
    peer_ids = jnp.arange(n_peers, dtype=jnp.int32)
    row_ids = jnp.arange(send_load.shape[0], dtype=jnp.int32)
    row_loads = jnp.sum(jnp.where(row_ids[:, None] == val_index, send_load, 0), axis=0)
    my_load = jnp.sum(jnp.where(peer_ids == my_index, row_loads, 0))
    slot_ranks = jnp.arange(slot_count, dtype=jnp.int32)
    slot_live = slot_ranks < my_load
    slot_tokens = tokens[0]
    slot_owner = owner[0]
    row_starts = jnp.cumsum(row_loads) - row_loads
    my_start = jnp.sum(jnp.where(peer_ids == my_index, row_starts, 0))
    target_offset = (peer_ids - my_start) % n_peers
    target_live = target_offset < my_load
    target_rank = jnp.minimum(target_offset, slot_count - 1)
    incoming_live = (my_index - row_starts) % n_peers < row_loads
    arrived_rank = jnp.cumsum(incoming_live.astype(jnp.int32))
    source_pick = jnp.sum(
        (arrived_rank[None, :] <= jnp.arange(evaluated, dtype=jnp.int32)[:, None]).astype(
            jnp.int32
        ),
        axis=1,
    )
    out_tokens = jnp.take(slot_tokens, target_rank, axis=0)
    out_local = jnp.take(slot_owner, target_rank, axis=0) // ITERS
    outgoing = build_states(out_tokens, out_local, tok_embed, board_context)
    outgoing = jnp.where(target_live[:, None, None], outgoing, 0.0).astype(jnp.bfloat16)
    arrived = lax.all_to_all(outgoing, "pos", split_axis=0, concat_axis=0, tiled=True)
    batch_states = jnp.take(arrived, source_pick, axis=0)
    values = encode(batch_states, w_qkv, w_attn_out, w_up, w_down, w_value)
    dest_of_slot = (my_start + slot_ranks) % n_peers
    source_hot = (source_pick[None, :] == peer_ids[:, None]).astype(jnp.float32)
    reply_rows = jnp.sum(source_hot[:, :, None] * values[None, :, :], axis=1)
    replies = lax.all_to_all(reply_rows, "pos", split_axis=0, concat_axis=0, tiled=True)
    dest_hot = (dest_of_slot[:, None] == peer_ids[None, :]).astype(jnp.float32)
    slot_values = jnp.sum(dest_hot[:, :, None] * replies[None, :, :], axis=1)
    slot_values = jnp.where(slot_live[:, None], slot_values, 0.0)
    cell_count = local_positions * ITERS
    cell_hot = (
        (slot_owner[:, None] == jnp.arange(cell_count, dtype=jnp.int32)[None, :])
        & slot_live[:, None]
    ).astype(jnp.float32)
    action_hot = (
        joint_action[0][:, :, None] == jnp.arange(ACTIONS, dtype=jnp.int32)[None, None, :]
    ).astype(jnp.float32)
    value_sums = jnp.einsum(
        "kc,kia->cia",
        cell_hot,
        action_hot * slot_values[:, :, None],
        precision=lax.Precision.HIGHEST,
    )
    counts = jnp.einsum("kc,kia->cia", cell_hot, action_hot, precision=lax.Precision.HIGHEST)
    value_sums, counts = lax.psum((value_sums, counts), "val")
    grid_shape = (local_positions, ITERS, POWERS, ACTIONS)
    avg_policy = regret_matching(value_sums.reshape(grid_shape), counts.reshape(grid_shape))
    return (slot_values[None], avg_policy)


def solution(mesh):
    in_specs = (
        P(),
        P("val", "pos", None),
        P("val", "pos"),
        P("val", "pos", None),
        P("pos", None, None),
        P(),
        P(),
        P(),
        P(),
        P(),
        P(),
    )
    out_specs = (P("val", "pos", None), P("pos", None, None))
    return jax.shard_map(local, mesh=mesh, in_specs=in_specs, out_specs=out_specs, check_vma=False)
```

profile of v0, /device:TPU:0, one launch (start us, length us, event | category | flops | bytes accessed | tf_op | source)
XLA Modules:
  0.0 96.5 jit_solution(931027213098821537)
XLA Ops:
  0.7 0.9 select_reduce_fusion
  1.8 0.6 fusion.96
  2.4 0.8 fusion.64
  3.2 1.3 %compare_and_fusion = (pred[16]{0:T(512)(128)(4,1)S(1)}, pred[16]{0:T(512)(128)(4,1)S(1)}) fusion(s32[]{:T(128)} %get-tuple-element.11, s32[]{:T(128)} %get-tuple-element.10), kind=kLoop, calls=%fused_computation.170 | loop fusion | flops 320 | bytes 40 | tf_op jit(solution)/shard_map/jit(_take)/and | solution.py:129
  4.5 1.3 %gather_fusion = s32[16,81]{1,0:T(8,128)S(1)} fusion(s32[16,81]{1,0:T(8,128)} %bitcast.142, s32[1024]{0:T(1024)S(1)} %pad_clamp_fusion.1), kind=kCustom, calls=%fused_computation | custom fusion | bytes 10432 | tf_op jit(solution)/shard_map/jit(_take)/gather | solution.py:129
  5.8 1.3 %gather_fusion.1 = s32[16]{0:T(128)S(1)} fusion(s32[16]{0:T(128)} %bitcast.136, s32[1024]{0:T(1024)S(1)} %pad_clamp_fusion.1), kind=kCustom, calls=%fused_computation.1 | custom fusion | bytes 192 | tf_op jit(solution)/shard_map/jit(_take)/gather | solution.py:130
  7.1 0.7 and_select_fusion
  7.9 1.5 %fusion.90 = f32[16,81,512]{2,0,1:T(8,128)S(1)} fusion(bf16[2,81,512]{2,0,1:T(2,128)(2,1)} %param.15, s32[16]{0:T(128)S(1)} %and_select_fusion), kind=kOutput, calls=%fused_computation.166 | convolution fusion | flops 2654240 | bytes 2820160 | tf_op jit(solution)/shard_map/np,pld->nld/dot_general | solution.py:22
  9.4 3.1 %fusion.8 = bf16[16,81,512]{2,1,0:T(8,128)(2,1)} fusion(f32[16,81,512]{2,0,1:T(8,128)S(1)} %fusion.90, pred[16]{0:T(512)(128)(4,1)S(1)} %get-tuple-element.38, s32[16,81]{1,0:T(8,128)S(1)} %broadcast_select_fusion.1, bf16[64,512]{1,0:T(8,128)(2,1)S(1)} %copy-done.3), kind=kOutput, calls=%fused_computation.12 | convolution fusion | flops 87008256 | bytes 4052048 | tf_op jit(solution)/shard_map/nlv,vd->nld/dot_general | solution.py:22
  12.6 8.4 %all-to-all-start = ((bf16[16,81,512]{2,1,0:T(8,128)(2,1)}), bf16[16,81,512]{2,1,0:T(8,128)(2,1)S(1)}, u32[]{:S(2)}, u32[]{:S(2)}) async-start(bf16[16,81,512]{2,1,0:T(8,128)(2,1)} %fusion.8), calls=%async_computation | async-start | bytes 2883584 | tf_op jit(solution)/shard_map/all_to_all | solution.py:133
  21.2 0.7 and_select_fusion.2
  21.9 0.7 iota_compare_fusion.10
  22.9 29.9 %all-to-all-done = bf16[16,81,512]{2,1,0:T(8,128)(2,1)S(1)} async-done(((bf16[16,81,512]{2,1,0:T(8,128)(2,1)}), bf16[16,81,512]{2,1,0:T(8,128)(2,1)S(1)}, u32[]{:S(2)}, u32[]{:S(2)}) %all-to-all-start) | async-done | bytes 1327136 | tf_op jit(solution)/shard_map/all_to_all | solution.py:133
  54.0 0.8 convolution_convert_fusion
  54.8 0.8 fusion.120
  56.0 1.3 %copy.92 = bf16[4,81,512]{1,2,0:T(8,128)(2,1)S(1)} copy(bf16[4,81,512]{2,1,0:T(8,128)(2,1)} %get-tuple-element.14) | data formatting | bytes 663552 | tf_op jit(solution)/shard_map/reshape | solution.py:46
  57.3 1.0 %copy.90 = bf16[4,81,512]{1,2,0:T(8,128)(2,1)} copy(bf16[4,81,512]{2,1,0:T(8,128)(2,1)S(1)} %get-tuple-element.16) | data formatting | bytes 663552 | tf_op jit(solution)/shard_map/reshape | solution.py:49
  58.3 1.7 %fusion.10 = f32[4,8,81,81]{2,3,1,0:T(8,128)} fusion(bf16[4,81,8,64]{1,3,2,0:T(8,128)(2,1)S(1)} %bitcast.139, bf16[4,81,8,64]{1,3,2,0:T(8,128)(2,1)S(1)} %bitcast.140), kind=kOutput, calls=%fused_computation.17 | convolution fusion | flops 27083808 | bytes 1503360 | tf_op jit(solution)/shard_map/bqhe,bkhe->bhqk/dot_general | solution.py:22
  60.0 3.2 %convolution_convert_fusion.1 = bf16[4,8,64,81]{3,2,1,0:T(8,128)(2,1)} fusion(bf16[4,81,8,64]{1,3,2,0:T(8,128)(2,1)} %bitcast.141, f32[4,8,81,81]{2,3,1,0:T(8,128)} %fusion.10), kind=kOutput, calls=%fused_computation.27 | convolution fusion | flops 27462320 | bytes 1503360 | tf_op jit(solution)/shard_map/bhqk,bkhe->bqhe/dot_general | solution.py:22
  63.2 1.5 %fusion.122 = (f32[4,81]{1,0:T(4,128)S(1)}, f32[4,81,512]{2,1,0:T(8,128)S(1)}) fusion(bf16[4,81,512]{1,2,0:T(8,128)(2,1)} %bitcast.143, bf16[512,512]{1,0:T(8,128)(2,1)S(1)} %copy-done.2, bf16[4,81,512]{2,1,0:T(8,128)(2,1)S(1)} %gather_fusion.2, pred[4]{0:T(512)(128)(4,1)S(1)} %compare_and_fusion.1), kind=kOutput, calls=%fused_computation.211 | convolution fusion | flops 170532544 | bytes 1852692 | tf_op jit(solution)/shard_map/bld,de->ble/dot_general | solution.py:22
  65.0 2.7 %fusion.19 = f32[4,512]{1,0:T(4,128)S(1)} fusion(f32[4,81,512]{2,1,0:T(8,128)S(1)} %get-tuple-element.20, bf16[1024,512]{1,0:T(8,128)(2,1)} %param.20, bf16[512,1024]{1,0:T(8,128)(2,1)} %param.19, f32[4,81]{1,0:T(4,128)S(1)} %add_rsqrt_fusion, f32[4,81]{1,0:T(4,128)S(1)} %broadcast_multiply_fusion), kind=kOutput, calls=%fused_computation.30 | convolution fusion | flops 683290624 | bytes 2771488 | tf_op jit(solution)/shard_map/blf,fd->bld/dot_general | solution.py:22
  68.7 0.7 copy.76
  69.4 7.2 %all-to-all-start.1 = ((f32[16,1,7]{2,1,0:T(1,128)}), f32[16,1,7]{2,1,0:T(1,128)S(1)}, u32[]{:S(2)}, u32[]{:S(2)}) async-start(f32[16,1,7]{2,1,0:T(1,128)} %copy.76), calls=%async_computation.1 | async-start | bytes 16384 | tf_op jit(solution)/shard_map/all_to_all | solution.py:139
  76.6 7.2 %all-to-all-done.1 = f32[16,1,7]{2,1,0:T(1,128)S(1)} async-done(((f32[16,1,7]{2,1,0:T(1,128)}), f32[16,1,7]{2,1,0:T(1,128)S(1)}, u32[]{:S(2)}, u32[]{:S(2)}) %all-to-all-start.1) | async-done | bytes 480 | tf_op jit(solution)/shard_map/all_to_all | solution.py:139
  84.2 3.7 %all-reduce = (f32[16,7,32]{2,0,1:T(8,128)S(1)}, f32[16,7,32]{2,0,1:T(8,128)S(1)}) all-reduce(f32[16,7,32]{2,0,1:T(8,128)S(1)} %fusion.54, f32[16,7,32]{2,0,1:T(8,128)S(1)} %fusion.52), channel_id=1, replica_groups=mesh['pos'=16,'val'=2] {'val'}, use_global_device_ids=true, to_apply=%region_19.20 | all-reduce | flops 7168 | bytes 57344 | tf_op jit(solution)/shard_map/psum | solution.py:158
  89.1 1.0 %maximum_reduce_fusion.4 = (f32[2,7]{0,1:T(8,128)S(1)}, f32[2,7,32]{2,0,1:T(2,128)S(1)}) fusion(f32[2,8,7,32]{3,0,2,1:T(2,128)} %copy-done.4, f32[2,7]{0,1:T(8,128)S(1)} %broadcast_add_fusion.6, f32[2,7,32]{2,0,1:T(2,128)S(1)} %get-tuple-element.24), kind=kOutput, calls=%fused_computation.129 | output fusion | flops 3615 | bytes 34616 | tf_op jit(solution)/shard_map/sub | solution.py:84
  90.1 1.0 %maximum_reduce_fusion.3 = (f32[2,7]{0,1:T(8,128)S(1)}, f32[2,7,32]{2,0,1:T(2,128)S(1)}) fusion(f32[2,8,7,32]{3,0,2,1:T(2,128)} %copy-done.4, f32[2,7]{0,1:T(8,128)S(1)} %broadcast_add_fusion.5, f32[2,7,32]{2,0,1:T(2,128)S(1)} %get-tuple-element.26), kind=kOutput, calls=%fused_computation.128 | output fusion | flops 3615 | bytes 34616 | tf_op jit(solution)/shard_map/sub | solution.py:84
  91.1 1.0 %maximum_reduce_fusion.2 = (f32[2,7]{0,1:T(8,128)S(1)}, f32[2,7,32]{2,0,1:T(2,128)S(1)}) fusion(f32[2,8,7,32]{3,0,2,1:T(2,128)} %copy-done.4, f32[2,7]{0,1:T(8,128)S(1)} %broadcast_add_fusion.4, f32[2,7,32]{2,0,1:T(2,128)S(1)} %get-tuple-element.28), kind=kOutput, calls=%fused_computation.127 | output fusion | flops 3615 | bytes 34616 | tf_op jit(solution)/shard_map/sub | solution.py:84
  92.1 1.0 %maximum_reduce_fusion.1 = (f32[2,7]{0,1:T(8,128)S(1)}, f32[2,7,32]{2,0,1:T(2,128)S(1)}) fusion(f32[2,8,7,32]{3,0,2,1:T(2,128)} %copy-done.4, f32[2,7]{0,1:T(8,128)S(1)} %broadcast_add_fusion.3, f32[2,7,32]{2,0,1:T(2,128)S(1)} %get-tuple-element.30), kind=kOutput, calls=%fused_computation.126 | output fusion | flops 3615 | bytes 34616 | tf_op jit(solution)/shard_map/sub | solution.py:84
  93.2 1.0 %maximum_reduce_fusion = (f32[2,7]{0,1:T(8,128)S(1)}, f32[2,7,32]{2,0,1:T(2,128)S(1)}) fusion(f32[2,8,7,32]{3,0,2,1:T(2,128)} %copy-done.4, f32[2,7]{0,1:T(8,128)S(1)} %broadcast_add_fusion.2, f32[2,7,32]{2,0,1:T(2,128)S(1)} %get-tuple-element.32), kind=kOutput, calls=%fused_computation.125 | output fusion | flops 3615 | bytes 34616 | tf_op jit(solution)/shard_map/sub | solution.py:84
  94.2 1.0 %fusion.124 = (f32[2,7]{0,1:T(8,128)S(1)}, f32[2,7,32]{2,0,1:T(2,128)S(1)}) fusion(f32[2,8,7,32]{3,0,2,1:T(2,128)} %copy-done.4, f32[2,7]{0,1:T(8,128)S(1)} %broadcast_add_fusion.1, f32[2,7,32]{2,0,1:T(2,128)S(1)} %get-tuple-element.34), kind=kOutput, calls=%fused_computation.213 | output fusion | flops 3615 | bytes 34616 | tf_op jit(solution)/shard_map/sub | solution.py:84
  95.8 0.7 fusion.72
  (68 shorter events, 5.8 us)
Async XLA Ops:
  0.6 53.4 %copy-start = (bf16[512,1536]{1,0:T(8,128)(2,1)S(1)}, bf16[512,1536]{1,0:T(8,128)(2,1)}, u32[]{:S(2)}) copy-start(bf16[512,1536]{1,0:T(8,128)(2,1)} %param.17) | copy-start | bytes 4718596
  7.1 2.3 %copy-start.3 = (bf16[64,512]{1,0:T(8,128)(2,1)S(1)}, bf16[64,512]{1,0:T(8,128)(2,1)}, u32[]{:S(2)}) copy-start(bf16[64,512]{1,0:T(8,128)(2,1)} %param.16) | copy-start | bytes 196612
  12.5 8.6 %copy-start.5 = (s32[1,16,7]{1,0,2:T(1,128)S(1)}, s32[1,16,7]{1,0,2:T(1,128)}, u32[]{:S(2)}) copy-start(s32[1,16,7]{1,0,2:T(1,128)} %param.14) | copy-start | bytes 1348
  12.5 10.2 %copy-start.1 = (s32[1,16]{1,0:T(1,128)S(1)}, s32[1,16]{1,0:T(1,128)}, u32[]{:S(2)}) copy-start(s32[1,16]{1,0:T(1,128)} %param.13) | copy-start | bytes 196
  12.6 40.3 %all-to-all-start = ((bf16[16,81,512]{2,1,0:T(8,128)(2,1)}), bf16[16,81,512]{2,1,0:T(8,128)(2,1)S(1)}, u32[]{:S(2)}, u32[]{:S(2)}) async-start(bf16[16,81,512]{2,1,0:T(8,128)(2,1)} %fusion.8), calls=%async_computation | async-start | bytes 2883584 | tf_op jit(solution)/shard_map/all_to_all | solution.py:133
  60.0 3.2 %copy-start.2 = (bf16[512,512]{1,0:T(8,128)(2,1)S(1)}, bf16[512,512]{1,0:T(8,128)(2,1)}, u32[]{:S(2)}) copy-start(bf16[512,512]{1,0:T(8,128)(2,1)} %param.18) | copy-start | bytes 1572868
  65.0 3.0 %copy-start.6 = (bf16[512,7]{0,1:T(8,128)(2,1)S(1)}, bf16[512,7]{0,1:T(8,128)(2,1)}, u32[]{:S(2)}) copy-start(bf16[512,7]{0,1:T(8,128)(2,1)} %param.21) | copy-start | bytes 21508
  69.4 14.4 %all-to-all-start.1 = ((f32[16,1,7]{2,1,0:T(1,128)}), f32[16,1,7]{2,1,0:T(1,128)S(1)}, u32[]{:S(2)}, u32[]{:S(2)}) async-start(f32[16,1,7]{2,1,0:T(1,128)} %copy.76), calls=%async_computation.1 | async-start | bytes 16384 | tf_op jit(solution)/shard_map/all_to_all | solution.py:139
  88.5 0.6 copy-start.4
where the time goes:
time: 97.4 us; the launch traced here: 96.5 us
  waiting for transfers between devices  37.1 us (38%)
  starting transfers between devices  15.6 us (16%)
  matrix products  15.3 us (16%)
  other arithmetic  15 us (15%)
  local copies, waits for them, and re-layouts  8.81 us (9%)
  blocking collectives  3.7 us (4%)
    all_to_all x1, waiting for transfers between devices, local(): lax.all_to_all(outgoing, 'pos', split_axis=0, concat_axis=0, tiled=True)  29.9 us
    dot_general x7, matrix products, multiply(): jnp.einsum(pattern, first_op, second_op, preferred_element_type=jnp.float32)  14.6 us
    all_to_all x1, starting transfers between devices, local(): lax.all_to_all(outgoing, 'pos', split_axis=0, concat_axis=0, tiled=True)  8.45 us
    all_to_all x1, waiting for transfers between devices, local(): lax.all_to_all(reply_rows, 'pos', split_axis=0, concat_axis=0, tiled=True)  7.19 us
    all_to_all x1, starting transfers between devices, local(): lax.all_to_all(reply_rows, 'pos', split_axis=0, concat_axis=0, tiled=True)  7.15 us
    sub x7, other arithmetic, regret_matching(): regrets = regrets + current - expected  6.22 us
    psum x1, blocking collectives, local(): value_sums, counts = lax.psum((value_sums, counts), 'val')  3.7 us
  transfers between devices with their start and end apart: 2, of which 2 were waited for; matrix products, arithmetic and copies ran while one was open for 2% of the time, Pallas kernels for 0%

commit v1 on v0

v1 whole, which is shorter than its diff:
```python
import functools
import math

import jax
import jax.numpy as jnp
from jax import lax
from jax.experimental import pallas as pl
from jax.experimental.pallas import tpu as pltpu
from jax.sharding import PartitionSpec as P

HEADS = 8
POWERS = 7
ACTIONS = 32
ITERS = 8
GROUP = 4
SMOOTHING = 0.01
F32 = jnp.float32
BF16 = jnp.bfloat16


def dot(a, b):
    return jnp.dot(a, b, preferred_element_type=F32)


def dot_nt(a, b):
    return lax.dot_general(a, b, (((1,), (1,)), ((), ())), preferred_element_type=F32)


def dot_tn(a, b):
    return lax.dot_general(a, b, (((0,), (0,)), ((), ())), preferred_element_type=F32)


def norm(u):
    centre = u - jnp.mean(u, axis=-1, keepdims=True)
    spread = jnp.mean(centre * centre, axis=-1, keepdims=True)
    return centre * lax.rsqrt(spread + 1e-05)


def span_of(load_ref, n_rows, pos, me):
    starts, total = [], jnp.int32(0)
    for v in range(n_rows):
        starts.append(total)
        total = total + load_ref[v, pos]
    low = lax.div(me * total + (n_rows - 1), jnp.int32(n_rows))
    high = lax.div((me + 1) * total + (n_rows - 1), jnp.int32(n_rows))
    return starts, low, high


def evaluate_kernel(n_rows, n_blocks, locs, *refs):
    load_ref = refs[0]
    owner_refs = refs[1 : 1 + n_blocks]
    token_refs = refs[1 + n_blocks : 1 + 2 * n_blocks]
    (
        board_ref,
        embed_ref,
        value_ref,
        qkv_hbm,
        out_hbm,
        up_hbm,
        down_hbm,
        result_ref,
        qkv_ref,
        out_ref,
        up_ref,
        down_ref,
        token_ref,
        state_ref,
        joined_ref,
        mixed_ref,
        hidden_sum,
        active_sum,
        sem,
    ) = refs[1 + 2 * n_blocks :]
    copies = [
        pltpu.make_async_copy(source, target, sem.at[i])
        for i, (source, target) in enumerate(
            (
                (qkv_hbm, qkv_ref),
                (out_hbm, out_ref),
                (up_hbm, up_ref),
                (down_hbm, down_ref),
            )
        )
    ]
    for copy in copies:
        copy.start()
    pos, me = lax.axis_index("pos"), lax.axis_index("val")
    width = embed_ref.shape[1]
    vocab = embed_ref.shape[0]
    pitch = state_ref.shape[0] // GROUP
    pad = pitch - locs
    slots = token_ref.shape[0] // n_rows
    starts, low, high = span_of(load_ref, n_rows, pos, me)
    count = high - low
    if n_blocks == 1:
        token_ref[...] = token_refs[0][...]
    else:
        for b in range(n_blocks):
            at = pl.multiple_of(lax.rem(me + b, n_rows) * slots, 8)
            token_ref[pl.ds(at, slots), :] = token_refs[b][...]
    state_ref[...] = jnp.zeros_like(state_ref)
    mixed_ref[...] = jnp.zeros_like(mixed_ref)
    head = width // HEADS
    pairs = HEADS // 2
    key_rows = 128
    lane = lax.broadcasted_iota(jnp.int32, (pitch, 2 * head), 1)
    first_half = lane < head
    key_gap = jnp.zeros((key_rows - pitch, 2 * head), F32)
    row_k = lax.broadcasted_iota(jnp.int32, (2 * key_rows, 2 * head), 0)
    lane_k = lax.broadcasted_iota(jnp.int32, (2 * key_rows, 2 * head), 1)
    ones_block = jnp.where(
        (lax.rem(row_k, key_rows) < locs) & ((row_k >= key_rows) == (lane_k >= head)), 1.0, 0.0
    ).astype(BF16)
    score_scale = head ** (-0.5) * math.log2(math.e)
    vocab_ids = lax.broadcasted_iota(jnp.int32, (vocab, locs), 0)

    def owner_at(row, slot):
        if n_blocks == 1:
            return owner_refs[0][row, slot]
        return jnp.where(row == me, owner_refs[0][0, slot], owner_refs[1][0, slot])

    copies[0].wait()
    copies[1].wait()
    copies[2].wait()

    def group_step(group, carry):
        places = []
        for g in range(GROUP):
            item = low + jnp.minimum(group * GROUP + g, count - 1)
            row, start = jnp.int32(0), jnp.int32(0)
            for v in range(1, n_rows):
                inside = item >= starts[v]
                row = jnp.where(inside, v, row)
                start = jnp.where(inside, starts[v], start)
            slot = item - start
            place = row * slots + slot
            places.append(place)
            board = lax.div(owner_at(row, slot), jnp.int32(ITERS))
            ids = token_ref[pl.ds(place, 1), :]
            hot = jnp.where(vocab_ids == ids, 1.0, 0.0).astype(BF16)
            state = dot_tn(hot, embed_ref[...]) + board_ref[board].astype(F32)
            state_ref[pl.ds(g * pitch, locs), :] = state.astype(BF16).astype(F32)
        states = state_ref[...]
        normed = norm(states).astype(BF16)
        joined_ref[...] = dot(normed, qkv_ref[...])
        for g in range(GROUP):
            rows = pl.ds(g * pitch, pitch)
            for p in range(pairs):
                at = p * 2 * head
                query = joined_ref[rows, at : at + 2 * head].astype(BF16)
                key = joined_ref[rows, width + at : width + at + 2 * head]
                value = joined_ref[rows, 2 * width + at : 2 * width + at + 2 * head] * (1.0 / 128.0)
                keys = jnp.concatenate(
                    [
                        jnp.where(first_half, key, 0.0),
                        key_gap,
                        jnp.where(first_half, 0.0, key),
                        key_gap,
                    ],
                    axis=0,
                ).astype(BF16)
                values = jnp.concatenate(
                    [
                        jnp.where(first_half, value, 0.0),
                        key_gap,
                        jnp.where(first_half, 0.0, value),
                        key_gap,
                    ],
                    axis=0,
                ).astype(BF16)
                weights = jnp.exp2(dot_nt(query, keys) * score_scale).astype(BF16)
                both = dot(weights, jnp.concatenate([values, ones_block], axis=1))
                part = both[:, : 2 * head] / both[:, 2 * head :] * 128.0
                mixed_ref[pl.ds(g * pitch, locs), at : at + 2 * head] = part[:locs]
        hidden = states + dot(mixed_ref[...].astype(BF16), out_ref[...])
        normed_two = norm(hidden).astype(BF16)
        for g in range(GROUP):
            part = hidden[g * pitch : (g + 1) * pitch]
            hidden_sum[pl.ds(places[g], 1), :] = jnp.sum(part, axis=0, keepdims=True)
        chunk = 256
        for c in range(up_ref.shape[1] // chunk):
            up = dot(normed_two, up_ref[:, c * chunk : (c + 1) * chunk])
            inner = up * (
                math.sqrt(2.0 / math.pi) + (math.sqrt(2.0 / math.pi) * 0.044715) * (up * up)
            )
            half = 0.5 * up
            active = half + half * jnp.tanh(inner)
            for g in range(GROUP):
                part = active[g * pitch : (g + 1) * pitch]
                active_sum[pl.ds(places[g], 1), c * chunk : (c + 1) * chunk] = jnp.sum(
                    part, axis=0, keepdims=True
                )
        return carry

    lax.fori_loop(0, lax.div(count + (GROUP - 1), jnp.int32(GROUP)), group_step, 0)
    copies[3].wait()
    places = result_ref.shape[0]
    place_ids = lax.broadcasted_iota(jnp.int32, (places, 1), 0)
    mine = place_ids < 0
    for v in range(n_rows):
        item = place_ids - v * slots + starts[v]
        inside = (place_ids >= v * slots) & (place_ids - v * slots < load_ref[v, pos])
        mine = mine | (inside & (item >= low) & (item < high))
    active = jnp.where(mine, active_sum[...], 0.0)
    active_high = active.astype(BF16)
    active_low = (active - active_high.astype(F32)).astype(BF16)
    final = (
        jnp.where(mine, hidden_sum[...], 0.0)
        + dot(active_high, down_ref[...])
        + dot(active_low, down_ref[...])
    )
    pooled = norm(final * (1.0 / locs)).astype(BF16)
    raised = jnp.exp(2.0 * dot(pooled, value_ref[...]))
    values = raised / jnp.sum(raised, axis=-1, keepdims=True)
    result_ref[...] = jnp.where(mine, values, 0.0)


def finish_kernel(n_rows, n_blocks, n_values, *refs):
    load_ref = refs[0]
    owner_refs = refs[1 : 1 + n_blocks]
    action_refs = refs[1 + n_blocks : 1 + 2 * n_blocks]
    value_refs = refs[1 + 2 * n_blocks : 1 + 2 * n_blocks + n_values]
    state_values_ref, policy_ref, value_ref = refs[1 + 2 * n_blocks + n_values :]
    pos, me = lax.axis_index("pos"), lax.axis_index("val")
    slots = state_values_ref.shape[0]
    boards = policy_ref.shape[0]
    total = value_refs[0][...]
    for r in value_refs[1:]:
        total = total + r[...]
    value_ref[...] = total
    state_values_ref[...] = value_ref[pl.ds(pl.multiple_of(me * slots, 8), slots), :]
    lanes = 128
    stride = boards * POWERS
    lane = lax.broadcasted_iota(jnp.int32, (slots, lanes), 1)
    lane_iter = lax.div(lane, jnp.int32(stride))
    lane_board = lax.div(lax.rem(lane, jnp.int32(stride)), jnp.int32(POWERS))
    lane_power = lax.rem(lane, jnp.int32(POWERS))
    lane_cell = jnp.where(lane < ITERS * stride, lane_board * ITERS + lane_iter, -1)
    slot_down = lax.broadcasted_iota(jnp.int32, (slots, 1), 0)
    square = lax.broadcasted_iota(jnp.int32, (slots, slots), 0) == lax.broadcasted_iota(
        jnp.int32, (slots, slots), 1
    )
    action_ids = lax.broadcasted_iota(jnp.int32, (slots, ACTIONS), 1)
    hots, rights = [], []
    for v in range(n_rows):
        if n_blocks == 1:
            row = jnp.int32(v)
            owners = owner_refs[0][v : v + 1, :]
            actions = action_refs[0][v * slots : (v + 1) * slots, :]
        else:
            row = lax.rem(me + v, n_rows)
            owners = owner_refs[v][...]
            actions = action_refs[v][...]
        values = value_ref[pl.ds(pl.multiple_of(row * slots, 8), slots), :]
        cell = jnp.sum(jnp.where(square, owners, 0), axis=1, keepdims=True)
        cell_hot = (lane_cell == cell) & (slot_down < load_ref[row, pos])
        for i in range(POWERS):
            hots.append(jnp.where(actions[:, i : i + 1] == action_ids, 1.0, 0.0))
            here = cell_hot & (lane_power == i)
            amount = jnp.where(here, values[:, i : i + 1], 0.0)
            high = amount.astype(BF16).astype(F32)
            rest = amount - high
            middle = rest.astype(BF16).astype(F32)
            rights.append(
                jnp.concatenate(
                    [jnp.where(here, 1.0, 0.0), high, middle, rest - middle], axis=1
                )
            )
    sums = dot_tn(
        jnp.concatenate(hots, axis=0).astype(BF16), jnp.concatenate(rights, axis=0).astype(BF16)
    )
    counts = sums[:, :lanes]
    value_sums = sums[:, lanes : 2 * lanes] + (
        sums[:, 2 * lanes : 3 * lanes] + sums[:, 3 * lanes :]
    )
    visits = jnp.sum(counts, axis=0, keepdims=True)
    totals = jnp.sum(value_sums, axis=0, keepdims=True)
    baseline = (totals + 1.0 / POWERS) / (visits + 1.0)
    payoff = (value_sums + baseline) / (counts + 1.0)
    regrets = jnp.zeros((ACTIONS, lanes), F32)
    average = jnp.zeros((ACTIONS, lanes), F32)
    for t in range(ITERS):
        positive = jnp.maximum(regrets, 0.0)
        policy = (positive + SMOOTHING) / (
            jnp.sum(positive, axis=0, keepdims=True) + ACTIONS * SMOOTHING
        )
        current = payoff if t == 0 else pltpu.roll(payoff, lanes - t * stride, 1)
        regrets = regrets + current - jnp.sum(policy * current, axis=0, keepdims=True)
        average = average + policy
    turned = (average / ITERS).T
    for b in range(boards):
        policy_ref[b] = turned[b * POWERS : (b + 1) * POWERS]


def local(
    send_load,
    tokens,
    owner,
    joint_action,
    board_context,
    tok_embed,
    w_qkv,
    w_attn_out,
    w_up,
    w_down,
    w_value,
):
    n_rows = lax.axis_size("val")
    slots, locs = tokens.shape[1:]
    boards = board_context.shape[0]
    width, hidden_units = w_up.shape
    tokens = tokens.reshape(slots, locs)
    joint_action = joint_action.reshape(slots, POWERS)
    if n_rows == 2:

        def rows_of(array):
            return [array, lax.ppermute(array, "val", [(0, 1), (1, 0)])]

    else:

        def rows_of(array):
            return [lax.all_gather(array, "val", axis=0, tiled=True)]

    owners, token_blocks, actions = rows_of(owner), rows_of(tokens), rows_of(joint_action)
    n_blocks = len(owners)
    vmem = pl.BlockSpec(memory_space=pltpu.VMEM)
    smem = pl.BlockSpec(memory_space=pltpu.SMEM)
    hbm = pl.BlockSpec(memory_space=pl.ANY)
    pitch = -(-locs // 8) * 8
    places = n_rows * slots
    values = pl.pallas_call(
        functools.partial(evaluate_kernel, n_rows, n_blocks, locs),
        out_shape=jax.ShapeDtypeStruct((places, POWERS), F32),
        in_specs=[smem] + [smem] * n_blocks + [vmem] * n_blocks + [vmem] * 3 + [hbm] * 4,
        out_specs=vmem,
        scratch_shapes=[
            pltpu.VMEM(w_qkv.shape, BF16),
            pltpu.VMEM(w_attn_out.shape, BF16),
            pltpu.VMEM(w_up.shape, BF16),
            pltpu.VMEM(w_down.shape, BF16),
            pltpu.VMEM((places, locs), jnp.int32),
            pltpu.VMEM((GROUP * pitch, width), F32),
            pltpu.VMEM((GROUP * pitch, 3 * width), F32),
            pltpu.VMEM((GROUP * pitch, width), F32),
            pltpu.VMEM((places, width), F32),
            pltpu.VMEM((places, hidden_units), F32),
            pltpu.SemaphoreType.DMA((4,)),
        ],
        compiler_params=pltpu.CompilerParams(vmem_limit_bytes=40 * 1024 * 1024),
        name="evaluate",
    )(
        send_load,
        *owners,
        *token_blocks,
        board_context,
        tok_embed,
        w_value,
        w_qkv,
        w_attn_out,
        w_up,
        w_down,
    )
    if n_rows == 2:
        shares = [values, lax.ppermute(values, "val", [(0, 1), (1, 0)])]
    else:
        shares = [lax.psum(values, "val")]
    state_values, policy = pl.pallas_call(
        functools.partial(finish_kernel, n_rows, n_blocks, len(shares)),
        out_shape=(
            jax.ShapeDtypeStruct((slots, POWERS), F32),
            jax.ShapeDtypeStruct((boards, POWERS, ACTIONS), F32),
        ),
        in_specs=[smem] + [vmem] * (2 * n_blocks + len(shares)),
        out_specs=(vmem, vmem),
        scratch_shapes=[pltpu.VMEM((places, POWERS), F32)],
        compiler_params=pltpu.CompilerParams(vmem_limit_bytes=40 * 1024 * 1024),
        name="finish",
    )(send_load, *owners, *actions, *shares)
    return (state_values[None], policy)


def solution(mesh):
    in_specs = (
        P(),
        P("val", "pos", None),
        P("val", "pos"),
        P("val", "pos", None),
        P("pos", None, None),
        P(),
        P(),
        P(),
        P(),
        P(),
        P(),
    )
    out_specs = (P("val", "pos", None), P("pos", None, None))
    return jax.shard_map(local, mesh=mesh, in_specs=in_specs, out_specs=out_specs, check_vma=False)
```

time: 97.4 us -> 33 us (0.34)
  the two profiles are of different devices: /device:TPU:0 before, /device:TPU:13 now
where the time goes in v1:
time: 33 us; the launch traced here: 32.6 us
  Pallas kernels  18.4 us (56%)
  local copies, waits for them, and re-layouts  11 us (33%)
  starting transfers between devices  1.4 us (4%)
  waiting for transfers between devices  1.1 us (3%)
  between operations  0.71 us (2%)
    pallas_call x1, Pallas kernels, local(): pl.pallas_call(functools.partial(evaluate_kernel, n_rows, n_blocks, locs)...  17.2 us
    unnamed x26, local copies, waits for them, and re-layouts  10.9 us
    pallas_call x1, Pallas kernels, local(): pl.pallas_call(functools.partial(finish_kernel, n_rows, n_blocks, len(sha...  1.22 us
    ppermute x3, waiting for transfers between devices, rows_of(): return [array, lax.ppermute(array, 'val', [(0, 1), (1, 0)])]  1.1 us
    ppermute x3, starting transfers between devices, rows_of(): return [array, lax.ppermute(array, 'val', [(0, 1), (1, 0)])]  0.9 us
  transfers between devices with their start and end apart: 4, of which 1 were waited for; matrix products, arithmetic and copies ran while one was open for 6% of the time, Pallas kernels for 0%

profile of v1, /device:TPU:13, one launch (start us, length us, event | category | flops | bytes accessed | tf_op | source)
XLA Modules:
  0.0 32.6 jit_solution(6257559001601992861)
XLA Ops:
  0.6 0.7 %collective-permute-start.2 = (s32[16,81]{1,0:T(8,128)}, s32[16,81]{1,0:T(8,128)S(1)}, u32[]{:S(2)}, u32[]{:S(2)}) collective-permute-start(s32[16,81]{1,0:T(8,128)} %bitcast.5), channel_id=1, source_target_pairs={{0,1},{1,0},{2,3},{3,2},{4,5},{5,4},{6,7},{7,6},{8,9},{9,8},{10,11... | collective-permute-start | bytes 15560 | tf_op jit(solution)/shard_map/ppermute | solution.py:317
  1.4 0.1 collective-permute-start
  1.5 0.9 %copy.14.refs_5_ = bf16[2,81,512]{2,1,0:T(8,128)(2,1)S(1)} copy(bf16[2,81,512]{2,0,1:T(2,128)(2,1)} %param.15) | data formatting | bytes 331776 | tf_op args[4]
  2.4 0.0 copy-start.10
  2.4 0.0 copy-start.7
  2.4 0.0 copy-start.9
  2.4 0.9 %copy.15.refs_7_ = bf16[512,7]{1,0:T(8,128)(2,1)S(1)} copy(bf16[512,7]{0,1:T(8,128)(2,1)} %param.21) | data formatting | bytes 14336 | tf_op args[10]
  3.3 0.0 collective-permute-done.refs_2_
  3.3 0.0 collective-permute-done.2.refs_4_
  3.3 0.0 copy-start
  3.3 1.4 %copy-done = bf16[512,1536]{1,0:T(8,128)(2,1)S(1)} copy-done((bf16[512,1536]{1,0:T(8,128)(2,1)S(1)}, bf16[512,1536]{1,0:T(8,128)(2,1)}, u32[]{:S(2)}) %copy-start) | copy-done | bytes 1572888
  4.7 0.0 copy-start.1
  4.8 1.2 %copy-done.1 = bf16[512,1024]{1,0:T(8,128)(2,1)S(1)} copy-done((bf16[512,1024]{1,0:T(8,128)(2,1)S(1)}, bf16[512,1024]{1,0:T(8,128)(2,1)}, u32[]{:S(2)}) %copy-start.1) | copy-done | bytes 1048600
  6.0 0.0 copy-start.2
  6.0 1.2 %copy-done.2 = bf16[1024,512]{1,0:T(8,128)(2,1)S(1)} copy-done((bf16[1024,512]{1,0:T(8,128)(2,1)S(1)}, bf16[1024,512]{1,0:T(8,128)(2,1)}, u32[]{:S(2)}) %copy-start.2) | copy-done | bytes 1048600
  7.2 1.0 %copy-done.3 = bf16[512,512]{1,0:T(8,128)(2,1)S(1)} copy-done((bf16[512,512]{1,0:T(8,128)(2,1)S(1)}, bf16[512,512]{1,0:T(8,128)(2,1)}, u32[]{:S(2)}) %copy-start.3) | copy-done | bytes 524312
  8.2 0.8 %copy-done.4 = bf16[64,512]{1,0:T(8,128)(2,1)S(1)} copy-done((bf16[64,512]{1,0:T(8,128)(2,1)S(1)}, bf16[64,512]{1,0:T(8,128)(2,1)}, u32[]{:S(2)}) %copy-start.4) | copy-done | bytes 65560
  9.1 0.7 %copy-done.5 = s32[1,16,81]{2,1,0:T(8,128)S(1)} copy-done((s32[1,16,81]{2,1,0:T(8,128)S(1)}, s32[1,16,81]{2,1,0:T(8,128)}, u32[]{:S(2)}) %copy-start.5) | copy-done | bytes 5208
  9.8 0.7 %copy-done.6 = s32[2,16]{1,0:T(2,128)S(1)} copy-done((s32[2,16]{1,0:T(2,128)S(1)}, s32[2,16]{1,0:T(2,128)}, u32[]{:S(2)}) %copy-start.6) | copy-done | bytes 152
  10.5 0.7 %copy-done.8 = s32[1,16]{1,0:T(1,128)S(1)} copy-done((s32[1,16]{1,0:T(1,128)S(1)}, s32[1,16]{1,0:T(1,128)}, u32[]{:S(2)}) %copy-start.8) | copy-done | bytes 88
  11.1 17.2 %evaluate.1.refs_5_ = f32[32,7]{1,0:T(8,128)S(1)} custom-call(s32[2,16]{1,0:T(2,128)S(1)} %copy-done.6, s32[1,16]{1,0:T(1,128)S(1)} %copy-done.8, s32[1,16]{1,0:T(1,128)S(1)} %collective-permute-done.refs_2_, s32[16,81]{1,0:T(8,128)S(1)} %bitcast.6, s32[16,81]{1,0:T(8,128)S(1)} %collective-permute-done.2.refs_4_, bf16[2,81,512]{2,1,0:T(8,128)(2,1)S(1)} %copy.14.refs_5_, ...), custom_call_target="tpu_custom_call" | custom-call | tf_op jit(solution)/shard_map/evaluate/pallas_call | solution.py:331
  28.3 0.5 %collective-permute-start.3 = (f32[32,7]{1,0:T(8,128)S(1)}, f32[32,7]{1,0:T(8,128)S(1)}, u32[]{:S(2)}, u32[]{:S(2)}) collective-permute-start(f32[32,7]{1,0:T(8,128)S(1)} %evaluate.1.refs_5_), channel_id=1, source_target_pairs={{0,1},{1,0},{2,3},{3,2},{4,5},{5,4},{6,7},{7,6},{8,9},{9,8},{10,11... | collective-permute-start | bytes 2696 | tf_op jit(solution)/shard_map/ppermute | solution.py:364
  28.8 0.0 copy-done.10
  28.8 0.1 copy.20
  28.9 0.1 collective-permute-start.1
  28.9 1.1 %collective-permute-done.1.refs_4_ = s32[16,7]{1,0:T(8,128)S(1)} collective-permute-done((s32[16,7]{1,0:T(8,128)S(1)}, s32[16,7]{1,0:T(8,128)S(1)}, u32[]{:S(2)}, u32[]{:S(2)}) %collective-permute-start.1) | collective-permute-done | bytes 480 | tf_op jit(solution)/shard_map/ppermute | solution.py:317
  30.0 0.0 collective-permute-done.3.refs_6_
  30.0 0.0 copy-done.7
  30.0 0.0 copy-done.9
  30.0 1.2 %finish.1 = (f32[16,7]{1,0:T(8,128)S(1)}, f32[2,7,32]{2,1,0:T(8,128)S(1)}) custom-call(s32[2,16]{1,0:T(2,128)S(1)} %copy-done.7, s32[1,16]{1,0:T(1,128)S(1)} %copy-done.9, s32[1,16]{1,0:T(1,128)S(1)} %collective-permute-done.refs_2_, s32[16,7]{1,0:T(8,128)S(1)} %bitcast.4, s32[16,7]{1,0:T(8,128)S(1)} %collective-permute-done.1.refs_4_, ...), custom_call_target="tpu_custom_call" | custom-call | tf_op jit(solution)/shard_map/finish/pallas_call | solution.py:367
  31.3 0.6 %copy.19 = f32[2,7,32]{2,0,1:T(2,128)} copy(f32[2,7,32]{2,1,0:T(8,128)S(1)} %get-tuple-element.7) | data formatting | bytes 3584
  31.9 0.7 %copy.18 = f32[1,16,7]{1,0,2:T(1,128)} copy(f32[1,16,7]{2,1,0:T(8,128)S(1)} %bitcast.7) | data formatting | bytes 896
  (5 shorter events, 0.0 us)
Async XLA Ops:
  0.6 2.7 %collective-permute-start.2 = (s32[16,81]{1,0:T(8,128)}, s32[16,81]{1,0:T(8,128)S(1)}, u32[]{:S(2)}, u32[]{:S(2)}) collective-permute-start(s32[16,81]{1,0:T(8,128)} %bitcast.5), channel_id=1, source_target_pairs={{0,1},{1,0},{2,3},{3,2},{4,5},{5,4},{6,7},{7,6},{8,9},{9,8},{10,11... | collective-permute-start | bytes 15560 | tf_op jit(solution)/shard_map/ppermute | solution.py:317
  1.4 1.9 %collective-permute-start = (s32[1,16]{1,0:T(1,128)}, s32[1,16]{1,0:T(1,128)S(1)}, u32[]{:S(2)}, u32[]{:S(2)}) collective-permute-start(s32[1,16]{1,0:T(1,128)} %refs_1_.3), channel_id=1, source_target_pairs={{0,1},{1,0},{2,3},{3,2},{4,5},{5,4},{6,7},{7,6},{8,9},{9,8},{10,11... | collective-permute-start | bytes 200 | tf_op jit(solution)/shard_map/ppermute | solution.py:317
  2.4 26.4 %copy-start.10 = (s32[1,16,7]{1,0,2:T(1,128)S(1)}, s32[1,16,7]{1,0,2:T(1,128)}, u32[]{:S(2)}) copy-start(s32[1,16,7]{1,0,2:T(1,128)} %param.14) | copy-start | bytes 1348
  2.4 27.6 %copy-start.7 = (s32[2,16]{1,0:T(2,128)S(1)}, s32[2,16]{1,0:T(2,128)}, u32[]{:S(2)}) copy-start(s32[2,16]{1,0:T(2,128)} %refs_0_.3) | copy-start | bytes 388
  2.4 27.6 %copy-start.9 = (s32[1,16]{1,0:T(1,128)S(1)}, s32[1,16]{1,0:T(1,128)}, u32[]{:S(2)}) copy-start(s32[1,16]{1,0:T(1,128)} %refs_1_.3) | copy-start | bytes 196
  3.3 1.4 %copy-start = (bf16[512,1536]{1,0:T(8,128)(2,1)S(1)}, bf16[512,1536]{1,0:T(8,128)(2,1)}, u32[]{:S(2)}) copy-start(bf16[512,1536]{1,0:T(8,128)(2,1)} %refs_8_.1) | copy-start | bytes 4718596
  4.7 1.2 %copy-start.1 = (bf16[512,1024]{1,0:T(8,128)(2,1)S(1)}, bf16[512,1024]{1,0:T(8,128)(2,1)}, u32[]{:S(2)}) copy-start(bf16[512,1024]{1,0:T(8,128)(2,1)} %refs_10_.1) | copy-start | bytes 3145732
  6.0 1.2 %copy-start.2 = (bf16[1024,512]{1,0:T(8,128)(2,1)S(1)}, bf16[1024,512]{1,0:T(8,128)(2,1)}, u32[]{:S(2)}) copy-start(bf16[1024,512]{1,0:T(8,128)(2,1)} %refs_11_.1) | copy-start | bytes 3145732
  7.2 1.0 %copy-start.3 = (bf16[512,512]{1,0:T(8,128)(2,1)S(1)}, bf16[512,512]{1,0:T(8,128)(2,1)}, u32[]{:S(2)}) copy-start(bf16[512,512]{1,0:T(8,128)(2,1)} %refs_9_.1) | copy-start | bytes 1572868
  8.2 0.8 %copy-start.4 = (bf16[64,512]{1,0:T(8,128)(2,1)S(1)}, bf16[64,512]{1,0:T(8,128)(2,1)}, u32[]{:S(2)}) copy-start(bf16[64,512]{1,0:T(8,128)(2,1)} %refs_6_.1) | copy-start | bytes 196612
  9.1 0.7 %copy-start.5 = (s32[1,16,81]{2,1,0:T(8,128)S(1)}, s32[1,16,81]{2,1,0:T(8,128)}, u32[]{:S(2)}) copy-start(s32[1,16,81]{2,1,0:T(8,128)} %param.12) | copy-start | bytes 15556
  9.8 0.7 %copy-start.6 = (s32[2,16]{1,0:T(2,128)S(1)}, s32[2,16]{1,0:T(2,128)}, u32[]{:S(2)}) copy-start(s32[2,16]{1,0:T(2,128)} %refs_0_.3) | copy-start | bytes 388
  10.5 0.7 %copy-start.8 = (s32[1,16]{1,0:T(1,128)S(1)}, s32[1,16]{1,0:T(1,128)}, u32[]{:S(2)}) copy-start(s32[1,16]{1,0:T(1,128)} %refs_1_.3) | copy-start | bytes 196
  28.3 1.8 %collective-permute-start.3 = (f32[32,7]{1,0:T(8,128)S(1)}, f32[32,7]{1,0:T(8,128)S(1)}, u32[]{:S(2)}, u32[]{:S(2)}) collective-permute-start(f32[32,7]{1,0:T(8,128)S(1)} %evaluate.1.refs_5_), channel_id=1, source_target_pairs={{0,1},{1,0},{2,3},{3,2},{4,5},{5,4},{6,7},{7,6},{8,9},{9,8},{10,11... | collective-permute-start | bytes 2696 | tf_op jit(solution)/shard_map/ppermute | solution.py:364
  28.9 1.2 %collective-permute-start.1 = (s32[16,7]{1,0:T(8,128)S(1)}, s32[16,7]{1,0:T(8,128)S(1)}, u32[]{:S(2)}, u32[]{:S(2)}) collective-permute-start(s32[16,7]{1,0:T(8,128)S(1)} %bitcast.3), channel_id=1, source_target_pairs={{0,1},{1,0},{2,3},{3,2},{4,5},{5,4},{6,7},{7,6},{8,9},{9,8},{10,11... | collective-permute-start | bytes 1352 | tf_op jit(solution)/shard_map/ppermute | solution.py:317
